TPU v7x, 128 devices: a whole 4x4x4 slice. The times are simulated.
128 devices in a mesh: section: 8 (over z, y_lo), ctx: 16 (over x, y_hi, core).
Axes of the slice: x: 4, y: 4 (y_hi: 2, y_lo: 2; y = y_hi * 2 + y_lo), z: 4, core: 2. Of those that a mesh axis runs over, the one named last changes fastest.
Arguments:
- queries: bfloat16 [16, 2560, 3072], P('section', 'ctx'), may hold values from -28 to 28, as said below
- cotangent: bfloat16 [16, 2560, 3072], P('section', 'ctx'), may hold values from -6 to 6
- ret_query: bfloat16 [2560, 3072], P('ctx', 'section'), may hold values from -6 to 6
- ret_key: bfloat16 [2560, 3072], P('ctx', 'section'), may hold values from -6 to 6
- ret_value: bfloat16 [2560, 3072], P('ctx', 'section'), may hold values from -6 to 6
- gate_log: float32 [2560, 24], P('ctx', 'section'), may hold values from -1.5 to 0, as said below
- kv_weight: bfloat16 [3072, 2048], P('section'), may hold values from -0.109375 to 0.109375
Outputs:
- attention: bfloat16 [16, 2560, 3072], P('section', 'ctx')
- query_grad: bfloat16 [16, 2560, 3072], P('section', 'ctx')
- retention_grad: bfloat16 [2560, 3072], P('ctx', 'section')
Inputs may be any that keep to these rules, and one draw needn't show every extreme that they name: The attention queries are mostly of order one; a few rows may be scaled by up to 16. `gate_log`: every gate is below one.
All inputs are finite; a program needn't handle non-finite values.
Results may differ from a plain program's by a relative error of at most 0.034.
Values may be sent and summed in bfloat16 or wider, within the bound.
No kernel may reach another device: no remote copies, remote signals or barrier semaphores. Data moves between devices by JAX's collectives and lax.ppermute only.
A program may use at most 640 MiB of HBM per device.

v0:
```python
import math

import jax
import jax.numpy as jnp
from jax import lax
from jax.sharding import PartitionSpec as P

DH = 128


epsilon = 1e-06
highest = lax.Precision.HIGHEST


def entering(value, axis, join, neutral):
    count, mine = (lax.axis_size(axis), lax.axis_index(axis))
    pieces = jax.tree.map(lambda part: lax.all_gather(part, axis), value)
    running = jax.tree.map(
        lambda part, zero: jnp.full_like(part, 0) + jnp.asarray(zero, part.dtype), value, neutral
    )

    def lap(position, running):
        longer = join(running, jax.tree.map(lambda part: part[position], pieces))
        return jax.tree.map(lambda new, old: jnp.where(position < mine, new, old), longer, running)

    return lax.fori_loop(0, count - 1, lap, running)


def combine_state(earlier, later):
    return (earlier[0] * later[0], later[0][:, None, None] * earlier[1] + later[1])


def kept_memory_lines(ret_query, ret_key, ret_value, gate_log):
    row_count, heads_here = gate_log.shape
    head_width = ret_query.shape[1] // heads_here
    query_part = ret_query.astype(jnp.float32).reshape(row_count, heads_here, head_width)
    key_part = ret_key.astype(jnp.float32).reshape(row_count, heads_here, head_width)
    value_part = ret_value.astype(jnp.float32).reshape(row_count, heads_here, head_width)
    cumulative = jnp.cumsum(gate_log, axis=0)
    places = jnp.arange(row_count, dtype=jnp.int32)
    causal = places[:, None] >= places[None, :]
    spread = cumulative.T[:, :, None] - cumulative.T[:, None, :]
    weights = jnp.exp(jnp.where(causal[None], spread, -jnp.inf))
    scores = jnp.einsum("thd,uhd->htu", query_part, key_part, precision=highest)
    inside = jnp.einsum("htu,uhd->thd", weights * scores, value_part, precision=highest)
    tail_decay = jnp.exp(cumulative[-1][None, :] - cumulative)
    local_state = jnp.einsum("uh,uhd,uhe->hde", tail_decay, key_part, value_part, precision=highest)
    decay_total = jnp.exp(cumulative[-1])
    identity = (jnp.ones_like(decay_total), jnp.zeros_like(local_state))
    scanned = entering((decay_total, local_state), "ctx", combine_state, identity)
    state_before = scanned[1]
    carried = jnp.einsum("thd,hde->the", query_part, state_before, precision=highest)
    raw_output = inside + jnp.exp(cumulative)[:, :, None] * carried
    normed = raw_output * lax.rsqrt(
        jnp.mean(raw_output * raw_output, axis=-1, keepdims=True) + epsilon
    )
    return normed.astype(jnp.bfloat16).reshape(row_count, heads_here * head_width)


def cross_attention(query_rows, grad_rows, positions, full_cache):
    row_count, model_width = query_rows.shape
    kv_width = full_cache.shape[1] // 2
    head_width = DH
    kv_heads = kv_width // head_width
    group_size = model_width // kv_width
    total_rows = full_cache.shape[0]
    block_rows = math.gcd(512, total_rows)
    score_scale = 1.0 / math.sqrt(head_width)
    query_heads = query_rows.reshape(row_count, kv_heads, group_size, head_width)
    grad_heads = grad_rows.reshape(row_count, kv_heads, group_size, head_width)
    block_count = jnp.max(positions) // block_rows + 1

    def block_scores(block_index):
        first_row = block_index * block_rows
        cache_piece = lax.dynamic_slice_in_dim(full_cache, first_row, block_rows, 0)
        key_block = cache_piece[:, :kv_width].reshape(block_rows, kv_heads, head_width)
        value_block = cache_piece[:, kv_width:].reshape(block_rows, kv_heads, head_width)
        scores = (
            jnp.einsum("rkgd,ukd->kgru", query_heads, key_block, preferred_element_type=jnp.float32)
            * score_scale
        )
        visible = (
            positions[:, None] >= (first_row + jnp.arange(block_rows, dtype=jnp.int32))[None, :]
        )
        return (jnp.where(visible, scores, -jnp.inf), key_block, value_block)

    def stat_step(block_index, carried):
        row_top, row_total = carried
        scores = block_scores(block_index)[0]
        new_top = jnp.maximum(row_top, jnp.max(scores, axis=-1))
        row_total = row_total * jnp.exp(row_top - new_top) + jnp.sum(
            jnp.exp(scores - new_top[..., None]), axis=-1
        )
        return (new_top, row_total)

    start_top = jnp.full((kv_heads, group_size, row_count), -jnp.inf, jnp.float32)
    row_top, row_total = lax.fori_loop(
        0, block_count, stat_step, (start_top, jnp.zeros_like(start_top))
    )

    def soft_of(scores):
        return jnp.exp(scores - row_top[..., None]) / row_total[..., None]

    def forward_step(block_index, accumulated):
        scores, _, value_block = block_scores(block_index)
        probs_low = soft_of(scores).astype(jnp.bfloat16)
        return accumulated + jnp.einsum(
            "kgru,ukd->rkgd", probs_low, value_block, preferred_element_type=jnp.float32
        )

    start_out = jnp.zeros((row_count, kv_heads, group_size, head_width), jnp.float32)
    mixed_output = lax.fori_loop(0, block_count, forward_step, start_out).astype(jnp.bfloat16)
    row_delta = jnp.einsum(
        "rkgd,rkgd->kgr", grad_heads, mixed_output, preferred_element_type=jnp.float32
    )

    def backward_step(block_index, carried):
        query_grad, cache_term = carried
        scores, key_block, value_block = block_scores(block_index)
        soft_probs = soft_of(scores)
        probs_low = soft_probs.astype(jnp.bfloat16)
        prob_grad = jnp.einsum(
            "rkgd,ukd->kgru", grad_heads, value_block, preferred_element_type=jnp.float32
        )
        score_grad = (soft_probs * (prob_grad - row_delta[..., None]) * score_scale).astype(
            jnp.bfloat16
        )
        query_grad = query_grad + jnp.einsum(
            "kgru,ukd->rkgd", score_grad, key_block, preferred_element_type=jnp.float32
        )
        key_grad = jnp.einsum(
            "kgru,rkgd->ukd", score_grad, query_heads, preferred_element_type=jnp.float32
        )
        value_grad = jnp.einsum(
            "kgru,rkgd->ukd", probs_low, grad_heads, preferred_element_type=jnp.float32
        )
        rows_term = jnp.concatenate(
            [key_grad.reshape(block_rows, kv_width), value_grad.reshape(block_rows, kv_width)],
            axis=1,
        )
        first_row = block_index * block_rows
        before = lax.dynamic_slice_in_dim(cache_term, first_row, block_rows, 0)
        cache_term = lax.dynamic_update_slice_in_dim(cache_term, before + rows_term, first_row, 0)
        return (query_grad, cache_term)

    start_term = jnp.zeros((total_rows, 2 * kv_width), jnp.float32)
    query_grad, cache_term = lax.fori_loop(0, block_count, backward_step, (start_out, start_term))
    return (
        mixed_output.reshape(row_count, model_width),
        query_grad.astype(jnp.bfloat16).reshape(row_count, model_width),
        cache_term,
    )


def body(queries, cotangent, ret_query, ret_key, ret_value, gate_log, kv_weight):
    ret_out = kept_memory_lines(ret_query, ret_key, ret_value, gate_log)
    partial_rows = jnp.dot(ret_out, kv_weight, preferred_element_type=jnp.float32)
    cache = lax.psum(partial_rows, "section").astype(jnp.bfloat16)
    full_cache = lax.all_gather(cache, "ctx", axis=0, tiled=True)
    layer_count, own_count, model_width = queries.shape
    ctx_place = lax.axis_index("ctx")
    local_rows = jnp.arange(own_count, dtype=jnp.int32)
    total_rows = full_cache.shape[0]
    term_width = full_cache.shape[1]
    cache_total = jnp.zeros((total_rows, term_width), jnp.float32)
    attended_list = []
    grad_list = []
    positions = ctx_place * own_count + local_rows
    for layer in range(layer_count):
        mixed_output, query_grad, cache_term = cross_attention(
            queries[layer], cotangent[layer], positions, full_cache
        )
        cache_total = cache_total + cache_term
        attended_list.append(mixed_output)
        grad_list.append(query_grad)
    attended_all = jnp.stack(attended_list, axis=0)
    grad_rows_all = jnp.stack(grad_list, axis=0)
    own_part = lax.psum_scatter(cache_total, "ctx", scatter_dimension=0, tiled=True)
    summed_grad = lax.psum(own_part, "section")
    cache_grad = summed_grad.astype(jnp.bfloat16)
    retention_grad = jnp.einsum(
        "rw,cw->rc", cache_grad, kv_weight, preferred_element_type=jnp.float32
    ).astype(jnp.bfloat16)
    return (attended_all, grad_rows_all, retention_grad)


def solution(mesh):
    return jax.shard_map(
        body,
        mesh=mesh,
        in_specs=(
            P("section", "ctx", None),
            P("section", "ctx", None),
            P("ctx", "section"),
            P("ctx", "section"),
            P("ctx", "section"),
            P("ctx", "section"),
            P("section", None),
        ),
        out_specs=(P("section", "ctx", None), P("section", "ctx", None), P("ctx", "section")),
        check_vma=False,
    )
```

profile of v0, /device:TPU:0, one launch (start us, length us, event | category | flops | bytes accessed | tf_op | source)
XLA Modules:
  0.0 909.1 jit_solution(14526820011012768127)
XLA Ops:
  13.2 24.3 %all-gather.1 = f32[16,1,3]{2,1,0:T(1,128)S(1)} all-gather(f32[1,1,3]{2,1,0:T(1,128)S(1)} %bitcast.403), channel_id=1, replica_groups=mesh['section'=8,'ctx'=16] {'ctx'}, dimensions={0}, use_global_device_ids=true | all-gather | bytes 204 | tf_op jit(solution)/shard_map/all_gather | solution.py:17
  38.7 29.3 %all-gather.7.cloned.1.call-done = f32[48,128,128]{2,1,0:T(8,128)} async-done(((f32[3,128,128]{2,1,0:T(8,128)}), f32[48,128,128]{2,1,0:T(8,128)}) %all-gather.7.cloned.1.call-update) | async-done | bytes 3145744 | tf_op jit(solution)/shard_map/all_gather | solution.py:17
  68.0 16.0 %while.94 = (s32[]{:T(128)}, f32[3,128,128]{2,1,0:T(8,128)S(1)}, s32[]{:T(128)}, f32[16,3]{1,0:T(8,128)S(1)}, f32[16,3,128,128]{3,2,1,0:T(8,128)}, /*index=5*/s32[]{:T(128)}, s32[]{:T(128)}) while((s32[]{:T(128)}, f32[3,128,128]{2,1,0:T(8,128)S(1)}, s32[]{:T(128)}, f32[16,3]{1,0:T(8,128)S(1)}, f32[16,3,128,128]{3,2,1,0:T(8,128)}, ...), condition=%wide.region_4.5_spmd.clone, body=%wide.region_3.4_spmd.clone.sunk | while | flops 196612 | bytes 589973 | solution.py:26
  86.5 80.1 %all-reduce.3 = bf16[160,2048]{1,0:T(8,128)(2,1)} all-reduce(f32[160,2048]{1,0:T(8,128)} %fusion.63), channel_id=1, replica_groups=mesh['section'=8,'ctx'=16] {'section'}, use_global_device_ids=true, to_apply=%region_6.7 | all-reduce | flops 327680 | bytes 1966080 | tf_op jit(solution)/shard_map/psum | solution.py:158
  182.6 3.9 reshape_squeeze.14
  189.3 4.0 reshape_squeeze.15
  196.0 50.6 %all-gather.5.cloned.1.call-done = bf16[2560,2048]{1,0:T(8,128)(2,1)} async-done(((bf16[160,2048]{1,0:T(8,128)(2,1)}), bf16[2560,2048]{1,0:T(8,128)(2,1)}) %all-gather.5.cloned.1.call-update) | async-done | bytes 10485776 | tf_op jit(solution)/shard_map/all_gather | solution.py:159
  246.6 13.7 %copy.224 = bf16[2560,2048]{0,1:T(8,128)(2,1)} copy(bf16[2560,2048]{1,0:T(8,128)(2,1)} %all-gather.5.cloned.1.call-done) | data formatting | bytes 20971520
  261.6 5.9 while.88
  269.0 10.1 %while.89 = (s32[]{:T(128)}, f32[160,8,3,128]{3,0,2,1:T(8,128)}, s32[]{:T(128)}, bf16[2560,2048]{0,1:T(8,128)(2,1)}, bf16[160,8,3,128]{3,0,2,1:T(8,128)(2,1)S(1)...) while((s32[]{:T(128)}, f32[160,8,3,128]{3,0,2,1:T(8,128)}, ...), condition=%wide.region_12.13_spmd.clone, body=%wide.region_11.12_spmd.clone.sunk | while | flops 1017037504 | bytes 11406791 | solution.py:112
  273.0 6.1 bitcast_add_fusion.9
  284.2 6.0 while.90
  291.7 9.0 while.91
  294.8 5.8 bitcast_add_fusion.10
  313.2 9.6 %broadcast.119.clone = f32[2560,2048]{0,1:T(8,128)} broadcast(f32[]{:T(128)} %constant.132.clone.1), dimensions={} | broadcast | bytes 20971524 | tf_op jit(solution)/shard_map/broadcast.16
  322.8 14.2 %while.93 = (s32[]{:T(128)}, f32[160,8,3,128]{3,0,2,1:T(8,128)}, f32[2560,2048]{0,1:T(8,128)}, s32[]{:T(128)}, bf16[2560,2048]{0,1:T(8,128)(2,1)}, /*index=5*/bf...) while((s32[]{:T(128)}, f32[160,8,3,128]{3,0,2,1:T(8,128)}, ...), condition=%wide.region_22.23_spmd.clone, body=%wide.region_21.22_spmd.clone.sunk | while | flops 2536948224 | bytes 83499624 | solution.py:147
  331.6 5.4 fusion.214
  338.5 9.6 %broadcast.119.clone.1 = f32[2560,2048]{0,1:T(8,128)} broadcast(f32[]{:T(128)} %constant.132.clone.1), dimensions={} | broadcast | bytes 20971524 | tf_op jit(solution)/shard_map/broadcast.16
  348.2 14.4 %while.92 = (s32[]{:T(128)}, f32[160,8,3,128]{3,0,2,1:T(8,128)}, f32[2560,2048]{0,1:T(8,128)}, s32[]{:T(128)}, bf16[2560,2048]{0,1:T(8,128)(2,1)}, /*index=5*/bf...) while((s32[]{:T(128)}, f32[160,8,3,128]{3,0,2,1:T(8,128)}, ...), condition=%wide.region_20.21_spmd.clone, body=%wide.region_19.20_spmd.clone.sunk | while | flops 2536948224 | bytes 83499624 | solution.py:147
  357.1 5.3 fusion.198
  362.6 22.5 %add.195 = f32[2560,2048]{0,1:T(8,128)} add(f32[2560,2048]{0,1:T(8,128)} %get-tuple-element.388, f32[2560,2048]{0,1:T(8,128)} %get-tuple-element.389) | non-fusion elementwise | flops 5242880 | bytes 62914560 | tf_op jit(solution)/shard_map/add | solution.py:173
  385.1 21.3 %copy.295 = f32[2560,2048]{1,0:T(8,128)} copy(f32[2560,2048]{0,1:T(8,128)} %add.195) | data formatting | bytes 41943040
  434.5 372.6 %reduce-scatter.4.cloned.1.call-done = f32[160,2048]{1,0:T(8,128)} async-done(((f32[2560,2048]{1,0:T(8,128)}), f32[160,2048]{1,0:T(8,128)}) %reduce-scatter.4.cloned.1.call-update) | async-done | bytes 1310736
  809.8 89.9 %all-reduce.4 = bf16[160,2048]{0,1:T(8,128)(2,1)} all-reduce(f32[160,2048]{0,1:T(8,128)} %copy.296), channel_id=1, replica_groups=mesh['section'=8,'ctx'=16] {'section'}, use_global_device_ids=true, to_apply=%region_24.25 | all-reduce | flops 327680 | bytes 1966080 | tf_op jit(solution)/shard_map/psum | solution.py:179
  (197 shorter events, 136.4 us)
Async XLA Ops:
  7.2 77.7 %copy-start = (bf16[384,2048]{1,0:T(8,128)(2,1)S(1)}, bf16[384,2048]{1,0:T(8,128)(2,1)}, u32[]{:S(2)}) copy-start(bf16[384,2048]{1,0:T(8,128)(2,1)} %param.27) | copy-start | bytes 4718596
  7.2 77.2 %copy-start.27 = (bf16[160,384]{1,0:T(8,128)(2,1)S(1)}, bf16[160,384]{1,0:T(8,128)(2,1)}, u32[]{:S(2)}) copy-start(bf16[160,384]{1,0:T(8,128)(2,1)} %param.25) | copy-start | bytes 368644
  7.2 76.9 %copy-start.28 = (bf16[160,384]{1,0:T(8,128)(2,1)S(1)}, bf16[160,384]{1,0:T(8,128)(2,1)}, u32[]{:S(2)}) copy-start(bf16[160,384]{1,0:T(8,128)(2,1)} %param.23) | copy-start | bytes 368644
  7.2 60.8 %all-gather.7.cloned.1.call-start = ((), (), s32[]{:S(2)}) async-start(), calls=%async_computation.2 | async-start | bytes 3342336 | tf_op jit(solution)/shard_map/all_gather | solution.py:17
  13.2 233.5 %all-gather.5.cloned.1.call-start = ((), (), s32[]{:S(2)}) async-start(), calls=%async_computation.1 | async-start | bytes 11141120 | tf_op jit(solution)/shard_map/all_gather | solution.py:159
  166.6 640.5 %reduce-scatter.4.cloned.1.call-start = ((), (), s32[]{:S(2)}) async-start(), calls=%async_computation.3 | async-start | bytes 22282240
  264.5 2.3 copy-start.24
  279.1 5.1 copy-start.1
  287.2 2.3 copy-start.20
  291.7 3.2 copy-start.12
  291.7 3.2 copy-start.22
  300.6 3.7 copy-start.9
  300.6 3.7 copy-start.10
  313.2 9.6 %copy-start.4 = (bf16[160,8,3,128]{3,0,2,1:T(8,128)(2,1)S(1)}, bf16[160,8,3,128]{3,0,2,1:T(8,128)(2,1)}, u32[]{:S(2)}) copy-start(bf16[160,8,3,128]{3,0,2,1:T(8,128)(2,1)} %copy.238) | copy-start | bytes 2949124
  323.0 1.9 copy-start.13
  323.1 1.9 copy-start.23
  327.9 1.5 copy-start.7
  330.8 6.2 copy-start.8
  338.5 9.6 %copy-start.2 = (bf16[160,8,3,128]{3,0,2,1:T(8,128)(2,1)S(1)}, bf16[160,8,3,128]{3,0,2,1:T(8,128)(2,1)}, u32[]{:S(2)}) copy-start(bf16[160,8,3,128]{3,0,2,1:T(8,128)(2,1)} %copy-done.1) | copy-start | bytes 2949124
  338.5 9.6 %copy-start.3 = (bf16[160,8,3,128]{3,0,2,1:T(8,128)(2,1)S(1)}, bf16[160,8,3,128]{3,0,2,1:T(8,128)(2,1)}, u32[]{:S(2)}) copy-start(bf16[160,8,3,128]{3,0,2,1:T(8,128)(2,1)} %copy.234) | copy-start | bytes 2949124
  348.6 1.9 copy-start.15
  348.6 1.9 copy-start.26
  356.3 6.1 copy-start.6
  406.4 5.6 copy-start.17
  (8 other events, 8.7 us)
Sparse Core Ops, SparseCore 0:
  13.3 54.6 all-gather.6
  166.7 79.8 all-gather.4
  406.6 400.4 reduce-scatter.3
where the time goes:
time: 921 us; the launch traced here: 909 us
  waiting for transfers between devices  453 us (49%)
  blocking collectives  194 us (21%)
  local copies, waits for them, and re-layouts  131 us (14%)
  other arithmetic  76.7 us (8%)
  matrix products  36.2 us (4%)
  between operations  16.7 us (2%)
    unnamed x4, waiting for transfers between devices  373 us
    psum x1, blocking collectives, body(): summed_grad = lax.psum(own_part, 'section')  89.9 us
    psum x1, blocking collectives, body(): cache = lax.psum(partial_rows, 'section').astype(jnp.bfloat16)  80.1 us
    all_gather x1, waiting for transfers between devices, body(): full_cache = lax.all_gather(cache, 'ctx', axis=0, tiled=True)  50.6 us
    unnamed x30, local copies, waits for them, and re-layouts  48.1 us
    all_gather x1, waiting for transfers between devices, entering(): pieces = jax.tree.map(lambda part: lax.all_gather(part, axis), value)  29.3 us
    another operation x12, local copies, waits for them, and re-layouts  27.8 us
    all_gather x1, blocking collectives, entering(): pieces = jax.tree.map(lambda part: lax.all_gather(part, axis), value)  24.3 us
  transfers between devices with their start and end apart: 3, of which 3 were waited for; matrix products, arithmetic and copies ran while one was open for 6% of the time, Pallas kernels for 0%

commit v1 on v0

v1 whole, which is shorter than its diff:
```python
import functools
import math

import jax
import jax.numpy as jnp
from jax import lax
from jax.experimental import pallas as pl
from jax.experimental.pallas import tpu as pltpu
from jax.sharding import Mesh, PartitionSpec as P

F32 = jnp.float32
BF16 = jnp.bfloat16
DH = 128
TOK = 160
SECTION = ("z", "yl")
CTX = ("x", "yh", "core")
HEAD = ("x", "core")
BLOCK = ("z", "yl", "yh")
EVERY = SECTION + CTX
VMEM_LIMIT = 60 * 1024 * 1024
LOG2E = 1.4426950408889634
SCALE = 1.0 / math.sqrt(DH)
NT = (((1,), (1,)), ((), ()))
TN = (((0,), (0,)), ((), ()))


def transpose_pairs():
    pairs = []
    for s in range(8):
        for c in range(16):
            z, yl, yh = c // 4, (c // 2) % 2, c % 2
            x, core = s // 2, s % 2
            pairs.append((s * 16 + c, (z * 2 + yl) * 16 + x * 4 + yh * 2 + core))
    return pairs


TO_OWNER = transpose_pairs()
FROM_OWNER = [(b, a) for a, b in TO_OWNER]


def vmem(shape, dtype):
    return pltpu.VMEM(shape, dtype)


def whole():
    return pl.BlockSpec(memory_space=pltpu.VMEM)


def cumulate(gate):
    rows = gate.shape[0]
    lower = (
        lax.broadcasted_iota(jnp.int32, (rows, rows), 0)
        >= lax.broadcasted_iota(jnp.int32, (rows, rows), 1)
    ).astype(F32)
    return jnp.dot(lower, gate, precision=lax.Precision.HIGHEST, preferred_element_type=F32)


def split_rows(value):
    hi = value.astype(BF16)
    rest = value - hi.astype(F32)
    mid = rest.astype(BF16)
    low = (rest - mid.astype(F32)).astype(BF16)
    return hi, mid, low


def pack(packet_ref, states, logs):
    for h in range(3):
        packet_ref[h * DH : (h + 1) * DH, :] = states[h].astype(BF16)
    rows = []
    for h in range(3):
        rows.extend(split_rows(logs[h]))
    rows.append(jnp.zeros((7, DH), BF16))
    packet_ref[3 * DH :, :] = jnp.concatenate([r.astype(F32) for r in rows], axis=0).astype(BF16)


def unpack(packet_ref):
    states = [packet_ref[h * DH : (h + 1) * DH, :].astype(F32) for h in range(3)]
    tail = packet_ref[3 * DH :, :].astype(F32)
    logs = [tail[3 * h : 3 * h + 1] + tail[3 * h + 1 : 3 * h + 2] + tail[3 * h + 2 : 3 * h + 3] for h in range(3)]
    return states, logs


def local_state_kernel(k_ref, v_ref, gate_ref, packet_ref):
    cum = cumulate(gate_ref[...])
    last = cum[TOK - 1 : TOK, :]
    tail = jnp.exp(last - cum)
    states, logs = [], []
    for h in range(3):
        lanes = slice(h * DH, (h + 1) * DH)
        key = (k_ref[:, lanes].astype(F32) * tail[:, h : h + 1]).astype(BF16)
        states.append(lax.dot_general(key, v_ref[:, lanes], TN, preferred_element_type=F32))
        logs.append(jnp.broadcast_to(last[:, h : h + 1], (1, DH)))
    pack(packet_ref, states, logs)


def local_state(key, value, gate):
    return pl.pallas_call(
        local_state_kernel,
        out_shape=jax.ShapeDtypeStruct((3 * DH + 16, DH), BF16),
        in_specs=[whole()] * 3,
        out_specs=whole(),
    )(key, value, gate)


def group_kernel(place_ref, own_ref, a_ref, b_ref, c_ref, total_ref, prefix_ref):
    place = place_ref[0]
    parts = [unpack(r) for r in (own_ref, a_ref, b_ref, c_ref)]
    members = [place ^ k for k in range(4)]
    total_s, total_l, prefix_s, prefix_l = [], [], [], []
    for h in range(3):
        logs = [p[1][h] for p in parts]
        total = jnp.zeros((DH, DH), F32)
        prefix = jnp.zeros((DH, DH), F32)
        log_all = jnp.zeros((1, DH), F32)
        log_before = jnp.zeros((1, DH), F32)
        for j in range(4):
            after = jnp.zeros((1, DH), F32)
            between = jnp.zeros((1, DH), F32)
            for i in range(4):
                later = (members[i] > members[j]).astype(F32)
                after = after + logs[i] * later
                between = between + logs[i] * later * (members[i] < place).astype(F32)
            before = (members[j] < place).astype(F32)
            total = total + parts[j][0][h] * jnp.exp(after)
            prefix = prefix + parts[j][0][h] * (jnp.exp(between) * before)
            log_all = log_all + logs[j]
            log_before = log_before + logs[j] * before
        total_s.append(total)
        total_l.append(log_all)
        prefix_s.append(prefix)
        prefix_l.append(log_before)
    pack(total_ref, total_s, total_l)
    for h in range(3):
        prefix_ref[h] = prefix_s[h]
    prefix_ref[3] = jnp.concatenate(prefix_l + [jnp.zeros((DH - 3, DH), F32)], axis=0)


def group_totals(place, own, others):
    return pl.pallas_call(
        group_kernel,
        out_shape=[
            jax.ShapeDtypeStruct((3 * DH + 16, DH), BF16),
            jax.ShapeDtypeStruct((4, DH, DH), F32),
        ],
        in_specs=[pl.BlockSpec(memory_space=pltpu.SMEM)] + [whole()] * 4,
        out_specs=[whole()] * 2,
    )(place, own, *others)


def retention_kernel(place_ref, prefix_ref, a_ref, b_ref, c_ref, q_ref, k_ref, v_ref, gate_ref, w_ref, out_ref):
    place = place_ref[0]
    parts = [unpack(r) for r in (a_ref, b_ref, c_ref)]
    members = [lax.rem(place + 4 - k, 4) for k in range(1, 4)]
    cum = cumulate(gate_ref[...])
    cum_rows = jnp.concatenate([cum, jnp.zeros((TOK, DH - 3), F32)], axis=1).T
    causal = lax.broadcasted_iota(jnp.int32, (TOK, TOK), 0) >= lax.broadcasted_iota(
        jnp.int32, (TOK, TOK), 1
    )
    normed = []
    for h in range(3):
        lanes = slice(h * DH, (h + 1) * DH)
        logs = [p[1][h] for p in parts]
        before = jnp.zeros((DH, DH), F32)
        for j in range(3):
            between = jnp.zeros((1, DH), F32)
            for i in range(3):
                inside = jnp.logical_and(members[i] > members[j], members[i] < place).astype(F32)
                between = between + logs[i] * inside
            before = before + parts[j][0][h] * (jnp.exp(between) * (members[j] < place).astype(F32))
        state = before * jnp.exp(prefix_ref[3, h : h + 1, :]) + prefix_ref[h]
        column = cum[:, h : h + 1]
        spread = column - cum_rows[h : h + 1, :]
        weights = jnp.exp(jnp.where(causal, spread, -1e30))
        query = q_ref[:, lanes]
        scores = lax.dot_general(query, k_ref[:, lanes], NT, preferred_element_type=F32)
        raw = jnp.dot((weights * scores).astype(BF16), v_ref[:, lanes], preferred_element_type=F32)
        carried = jnp.dot(query, state.astype(BF16), preferred_element_type=F32)
        raw = raw + jnp.exp(column) * carried
        scale = lax.rsqrt(jnp.mean(raw * raw, axis=-1, keepdims=True) + 1e-6)
        normed.append((raw * scale).astype(BF16))
    rows = jnp.concatenate(normed, axis=1)
    for h in range(8):
        for part in range(2):
            lanes = slice(part * 8 * DH + h * DH, part * 8 * DH + (h + 1) * DH)
            out_ref[h, :, part * DH : (part + 1) * DH] = jnp.dot(
                rows, w_ref[:, lanes], preferred_element_type=F32
            ).astype(out_ref.dtype)


def retention(place, prefix, others, query, key, value, gate, weight):
    return pl.pallas_call(
        retention_kernel,
        out_shape=jax.ShapeDtypeStruct((8, TOK, 2 * DH), BF16),
        in_specs=[pl.BlockSpec(memory_space=pltpu.SMEM)] + [whole()] * 9,
        out_specs=whole(),
        compiler_params=pltpu.CompilerParams(vmem_limit_bytes=VMEM_LIMIT),
    )(place, prefix, *others, query, key, value, gate, weight)


CHUNK = 640
ROWS = 640
TK = 320


def attention_kernel(
    yh_ref, q_ref, do_ref, kv_ref, o_ref, dq_ref, dkv_ref, s_scr, p_scr, ds_scr, kt_scr, vt_scr, dk_acc, dv_acc
):
    step = pl.program_id(0)

    @pl.when(step == 0)
    def _():
        dk_acc[...] = jnp.zeros_like(dk_acc)
        dv_acc[...] = jnp.zeros_like(dv_acc)
        for b in range(4):
            rows = slice(b * CHUNK, (b + 1) * CHUNK)
            kt_scr[:, rows] = kv_ref[rows, :DH].astype(F32).T.astype(BF16)
            vt_scr[:, rows] = kv_ref[rows, DH:].astype(F32).T.astype(BF16)

    half = yh_ref[0] * 320
    lane = lax.broadcasted_iota(jnp.int32, (1, ROWS), 1)
    row_pos = half + TOK * (lane // 320) + lax.rem(lane, TOK)
    factor = SCALE * LOG2E
    for x in range(4):
        length = CHUNK * (x + 1)
        query = q_ref[2 * x : 2 * x + 2].reshape(ROWS, DH)
        grad = do_ref[2 * x : 2 * x + 2].reshape(ROWS, DH)

        def score_step(j, top):
            rows = pl.ds(pl.multiple_of(j * TK, TK), TK)
            s = lax.dot_general(kv_ref[rows, :DH], query, NT, preferred_element_type=F32)
            s_scr[rows, :] = s
            return jnp.maximum(top, jnp.max(s, axis=0, keepdims=True))

        def diag_step(j, top):
            rows = pl.ds(pl.multiple_of(x * CHUNK + j * TK, TK), TK)
            s = lax.dot_general(kv_ref[rows, :DH], query, NT, preferred_element_type=F32)
            key_pos = j * TK + lax.broadcasted_iota(jnp.int32, (TK, ROWS), 0)
            s = jnp.where(key_pos <= row_pos, s, -1e30)
            s_scr[rows, :] = s
            return jnp.maximum(top, jnp.max(s, axis=0, keepdims=True))

        top = jnp.full((1, ROWS), -1e30, F32)
        top = lax.fori_loop(0, x * CHUNK // TK, score_step, top)
        top = lax.fori_loop(0, CHUNK // TK, diag_step, top)
        top = top * factor

        def prob_step(j, total):
            rows = pl.ds(pl.multiple_of(j * TK, TK), TK)
            p = jnp.exp2(s_scr[rows, :] * factor - top)
            p_scr[rows, :] = p.astype(BF16)
            return total + jnp.sum(p, axis=0, keepdims=True)

        total = lax.fori_loop(0, length // TK, prob_step, jnp.zeros((1, ROWS), F32))
        inverse = 1.0 / total
        out_t = jnp.dot(vt_scr[:, :length], p_scr[:length, :], preferred_element_type=F32) * inverse
        out = out_t.T.astype(BF16)
        o_ref[2 * x : 2 * x + 2] = out.reshape(2, 2, TOK, DH)
        delta = jnp.sum((out.astype(F32) * grad.astype(F32)).T, axis=0, keepdims=True)
        inverse_col = jnp.broadcast_to(inverse, (DH, ROWS)).T
        grad_scaled = (grad.astype(F32) * inverse_col).astype(BF16)
        query_scaled = (query.astype(F32) * (inverse_col * SCALE)).astype(BF16)

        def grad_step(j, carry):
            rows = pl.ds(pl.multiple_of(j * TK, TK), TK)
            dp = lax.dot_general(kv_ref[rows, DH:], grad, NT, preferred_element_type=F32)
            p = p_scr[rows, :]
            ds = (p.astype(F32) * (dp - delta)).astype(BF16)
            ds_scr[rows, :] = ds
            dv_acc[rows, :] += jnp.dot(p, grad_scaled, preferred_element_type=F32)
            dk_acc[rows, :] += jnp.dot(ds, query_scaled, preferred_element_type=F32)
            return carry

        lax.fori_loop(0, length // TK, grad_step, 0)
        dq_t = jnp.dot(kt_scr[:, :length], ds_scr[:length, :], preferred_element_type=F32)
        dq = (dq_t * (inverse * SCALE)).T.astype(BF16)
        dq_ref[2 * x : 2 * x + 2] = dq.reshape(2, 2, TOK, DH)

    @pl.when(step == pl.num_programs(0) - 1)
    def _():
        dkv_ref[:, :DH] = dk_acc[...].astype(BF16)
        dkv_ref[:, DH:] = dv_acc[...].astype(BF16)


def attention_call(yh, queries, grads, cache):
    tokens = 4 * CHUNK
    by_head = pl.BlockSpec((8, 2, TOK, DH), lambda g: (0, 0, 0, g))
    const = pl.BlockSpec((tokens, 2 * DH), lambda g: (0, 0))
    return pl.pallas_call(
        attention_kernel,
        grid=(3,),
        out_shape=[
            jax.ShapeDtypeStruct((8, 2, TOK, 3 * DH), BF16),
            jax.ShapeDtypeStruct((8, 2, TOK, 3 * DH), BF16),
            jax.ShapeDtypeStruct((tokens, 2 * DH), BF16),
        ],
        in_specs=[pl.BlockSpec(memory_space=pltpu.SMEM), by_head, by_head, const],
        out_specs=[by_head, by_head, const],
        scratch_shapes=[
            vmem((tokens, ROWS), F32),
            vmem((tokens, ROWS), BF16),
            vmem((tokens, ROWS), BF16),
            vmem((DH, tokens), BF16),
            vmem((DH, tokens), BF16),
            vmem((tokens, DH), F32),
            vmem((tokens, DH), F32),
        ],
        compiler_params=pltpu.CompilerParams(vmem_limit_bytes=VMEM_LIMIT),
    )(yh, queries, grads, cache)


def project_kernel(g_ref, w_ref, out_ref):
    total = jnp.zeros(out_ref.shape, F32)
    for h in range(8):
        for part in range(2):
            lanes = slice(part * 8 * DH + h * DH, part * 8 * DH + (h + 1) * DH)
            total = total + lax.dot_general(
                g_ref[h, :, part * DH : (part + 1) * DH], w_ref[:, lanes], NT, preferred_element_type=F32
            )
    out_ref[...] = total.astype(BF16)


def project(grads, weight):
    return pl.pallas_call(
        project_kernel,
        out_shape=jax.ShapeDtypeStruct((TOK, weight.shape[0]), BF16),
        in_specs=[whole()] * 2,
        out_specs=whole(),
        compiler_params=pltpu.CompilerParams(vmem_limit_bytes=VMEM_LIMIT),
    )(grads, weight)


def exchange(value, axes):
    return lax.all_to_all(value, axes, 0, 0, tiled=True)


def gather_blocks(block, axes, count):
    return exchange(jnp.broadcast_to(block[None], (count,) + block.shape), axes)


def split_heads(rows):
    return rows.reshape(2, TOK, 8, 3 * DH).transpose(2, 0, 1, 3)


def join_heads(rows):
    return rows.transpose(1, 2, 0, 3).reshape(2, TOK, 24 * DH)


def body(queries, cotangent, ret_query, ret_key, ret_value, gate_log, kv_weight):
    x_place = lax.axis_index("x").astype(jnp.int32).reshape(1)
    yh_place = lax.axis_index("yh").astype(jnp.int32).reshape(1)
    in_group = (lax.axis_index("yh") * 2 + lax.axis_index("core")).astype(jnp.int32).reshape(1)
    q_heads = exchange(split_heads(queries), HEAD)
    do_heads = exchange(split_heads(cotangent), HEAD)

    packet = local_state(ret_key, ret_value, gate_log)
    near = [
        lax.ppermute(packet, ("yh", "core"), [(i, i ^ k) for i in range(4)]) for k in range(1, 4)
    ]
    total, prefix = group_totals(in_group, packet, near)
    far = [lax.ppermute(total, "x", [(i, (i + k) % 4) for i in range(4)]) for k in range(1, 4)]
    partial = retention(x_place, prefix, far, ret_query, ret_key, ret_value, gate_log, kv_weight)
    pieces = exchange(partial, SECTION)
    block = jnp.sum(pieces.astype(F32), axis=0).astype(BF16)
    block = lax.ppermute(block, EVERY, TO_OWNER)
    cache = gather_blocks(block, BLOCK, 16).reshape(16 * TOK, 2 * DH)

    attended, query_grad, cache_grad = attention_call(yh_place, q_heads, do_heads, cache)
    terms = exchange(cache_grad.reshape(16, TOK, 2 * DH), BLOCK)
    summed = jnp.sum(terms.astype(F32), axis=0).astype(BF16)
    summed = lax.ppermute(summed, EVERY, FROM_OWNER)
    grads = gather_blocks(summed, SECTION, 8)
    retention_grad = project(grads, kv_weight)
    attended = join_heads(exchange(attended, HEAD))
    query_grad = join_heads(exchange(query_grad, HEAD))
    return attended, query_grad, retention_grad


def solution(mesh):
    fine = Mesh(mesh.devices.reshape(4, 2, 4, 2, 2), EVERY)
    return jax.shard_map(
        body,
        mesh=fine,
        in_specs=(
            P(SECTION, CTX, None),
            P(SECTION, CTX, None),
            P(CTX, SECTION),
            P(CTX, SECTION),
            P(CTX, SECTION),
            P(CTX, SECTION),
            P(SECTION, None),
        ),
        out_specs=(P(SECTION, CTX, None), P(SECTION, CTX, None), P(CTX, SECTION)),
        check_vma=False,
    )
```

time: 921 us -> 322 us (0.35); the launches traced: 909 us -> 321 us
  waiting for transfers between devices: 453 us -> 104 us
  local copies, waits for them, and re-layouts: 131 us -> 15.3 us
  blocking collectives: 194 us -> 80.2 us
  Pallas kernels: 0 us -> 86.7 us
  other arithmetic: 76.7 us -> 0.28 us
  matrix products: 36.2 us -> 0 us
  starting transfers between devices: 0.12 us -> 34.3 us
  between operations: 16.7 us -> 0.75 us
    unnamed x4 -> x0, waiting for transfers between devices: 373 us -> none
    psum x2 -> x0, blocking collectives: 170 us -> none  [the longest x1 89.9 us: body(): summed_grad = lax.psum(own_part, 'section')]
    all_to_all x0 -> x5, waiting for transfers between devices: none -> 90.6 us  [exchange(): return lax.all_to_all(value, axes, 0, 0, tiled=True)]
    pallas_call x0 -> x5, Pallas kernels: none -> 86.7 us  [the longest x1 75 us: attention_call(): pl.pallas_call(attention_kernel, grid=(3,), out_shape=[jax.ShapeDtypeStru...]
    all_to_all x0 -> x3, blocking collectives: none -> 80.2 us  [exchange(): return lax.all_to_all(value, axes, 0, 0, tiled=True)]
    all_gather x2 -> x0, waiting for transfers between devices: 79.9 us -> none  [the longest x1 50.6 us: body(): full_cache = lax.all_gather(cache, 'ctx', axis=0, tiled=True)]
    another operation x20 -> x0, local copies, waits for them, and re-layouts: 53 us -> none
    unnamed x30 -> x21, local copies, waits for them, and re-layouts: 48.1 us -> 4.88 us
  transfers between devices with their start and end apart: 3 -> 13, of which waited for: 3 -> 10; matrix products, arithmetic and copies ran while one was open for 6% -> 3% of each run, Pallas kernels for 0% -> 0%
where the time goes in v1:
time: 322 us; the launch traced here: 321 us
  waiting for transfers between devices  104 us (32%)
  Pallas kernels  86.7 us (27%)
  blocking collectives  80.2 us (25%)
  starting transfers between devices  34.3 us (11%)
  local copies, waits for them, and re-layouts  15.3 us (5%)
    all_to_all x5, waiting for transfers between devices, exchange(): return lax.all_to_all(value, axes, 0, 0, tiled=True)  90.6 us
    all_to_all x3, blocking collectives, exchange(): return lax.all_to_all(value, axes, 0, 0, tiled=True)  80.2 us
    pallas_call x1, Pallas kernels, attention_call(): pl.pallas_call(attention_kernel, grid=(3,), out_shape=[jax.ShapeDtypeStru...  75 us
    all_to_all x5, starting transfers between devices, exchange(): return lax.all_to_all(value, axes, 0, 0, tiled=True)  25.1 us
    ppermute x3, waiting for transfers between devices, body(): lax.ppermute(total, 'x', [(i, (i + k) % 4) for i in range(4)])  6.54 us
    ppermute x3, waiting for transfers between devices, body(): lax.ppermute(packet, ('yh', 'core'), [(i, i ^ k) for i in range(4)])  6.5 us
  transfers between devices with their start and end apart: 13, of which 10 were waited for; matrix products, arithmetic and copies ran while one was open for 3% of the time, Pallas kernels for 0%

profile of v1, /device:TPU:0, one launch (start us, length us, event | category | flops | bytes accessed | tf_op | source)
XLA Modules:
  0.0 321.1 jit_solution(12181204166133640181)
XLA Ops:
  4.4 2.7 collective-permute-start.2
  7.8 3.2 collective-permute-done.2.c_ref
  11.0 3.3 %collective-permute-done.1.b_ref = bf16[400,128]{1,0:T(8,128)(2,1)S(1)} collective-permute-done((bf16[400,128]{1,0:T(8,128)(2,1)}, bf16[400,128]{1,0:T(8,128)(2,1)S(1)}, u32[]{:S(2)}, u32[]{:S(2)}) %collective-permute-start.1) | collective-permute-done | bytes 102432 | tf_op jit(solution)/shard_map/ppermute | solution.py:357
  16.9 2.7 collective-permute-start.5
  21.4 3.0 collective-permute-done.5.c_ref
  24.4 2.5 collective-permute-done.4.b_ref
  28.6 4.4 %shard_map.96 = bf16[8,160,256]{2,1,0:T(8,128)(2,1)} custom-call(s32[1]{0:T(128)} %bitcast.3.place_ref, f32[4,128,128]{2,1,0:T(8,128)} %get-tuple-element.8.prefix_ref, bf16[400,128]{1,0:T(8,128)(2,1)} %copy-done.9, bf16[400,128]{1,0:T(8,128)(2,1)} %copy-done.8, bf16[400,128]{1,0:T(8,128)(2,1)} %copy-done.7, bf16[160,384]{1,0:T(8,128)(2,1)} %q_ref.1, ...), custom_call_target="tpu_custom_call" | custom-call | tf_op jit(solution)/shard_map/pallas_call | solution.py:191
  33.0 5.7 %all-to-all-start.2 = ((bf16[8,160,256]{2,1,0:T(8,128)(2,1)}), bf16[8,160,256]{2,1,0:T(8,128)(2,1)S(1)}, u32[]{:S(2)}, u32[]{:S(2)}) async-start(bf16[8,160,256]{2,1,0:T(8,128)(2,1)} %shard_map.96), calls=%async_computation.2 | async-start | bytes 1310720 | tf_op jit(solution)/shard_map/all_to_all | solution.py:333
  40.2 9.7 %all-to-all-done.2 = bf16[8,160,256]{2,1,0:T(8,128)(2,1)S(1)} async-done(((bf16[8,160,256]{2,1,0:T(8,128)(2,1)}), bf16[8,160,256]{2,1,0:T(8,128)(2,1)S(1)}, u32[]{:S(2)}, u32[]{:S(2)}) %all-to-all-start.2) | async-done | bytes 655392 | tf_op jit(solution)/shard_map/all_to_all | solution.py:333
  49.9 3.6 %all-to-all-start = ((bf16[8,2,160,384]{3,2,1,0:T(8,128)(2,1)}), bf16[8,2,160,384]{3,2,1,0:T(8,128)(2,1)S(1)}, u32[]{:S(2)}, u32[]{:S(2)}) async-start(bf16[8,2,160,384]{3,2,1,0:T(8,128)(2,1)} %bitcast.27), calls=%async_computation | async-start | bytes 3932160 | tf_op jit(solution)/shard_map/all_to_all | solution.py:333
  53.5 3.1 copy.24
  56.6 22.6 %all-to-all-done.q_ref = bf16[8,2,160,384]{3,2,1,0:T(8,128)(2,1)S(1)} async-done(((bf16[8,2,160,384]{3,2,1,0:T(8,128)(2,1)}), bf16[8,2,160,384]{3,2,1,0:T(8,128)(2,1)S(1)}, u32[]{:S(2)}, u32[]{:S(2)}) %all-to-all-start) | async-done | bytes 1966112 | tf_op jit(solution)/shard_map/all_to_all | solution.py:333
  80.5 4.3 %all-to-all-start.1 = ((bf16[8,2,160,384]{3,2,1,0:T(8,128)(2,1)}), bf16[8,2,160,384]{3,2,1,0:T(8,128)(2,1)}, u32[]{:S(2)}, u32[]{:S(2)}) async-start(bf16[8,2,160,384]{3,2,1,0:T(8,128)(2,1)} %bitcast.26), calls=%async_computation.1 | async-start | bytes 3932160 | tf_op jit(solution)/shard_map/all_to_all | solution.py:333
  85.6 25.6 %all-to-all-done.1.do_ref = bf16[8,2,160,384]{3,2,1,0:T(8,128)(2,1)} async-done(((bf16[8,2,160,384]{3,2,1,0:T(8,128)(2,1)}), bf16[8,2,160,384]{3,2,1,0:T(8,128)(2,1)}, u32[]{:S(2)}, u32[]{:S(2)}) %all-to-all-start.1) | async-done | bytes 1966112 | tf_op jit(solution)/shard_map/all_to_all | solution.py:333
  111.3 29.4 %all_to_all.40 = bf16[16,160,256]{2,1,0:T(8,128)(2,1)} all-to-all(bf16[16,160,256]{2,1,0:T(8,128)(2,1)S(1)} %broadcast_in_dim.4), channel_id=1, replica_groups=mesh['z'=4,'yl'=2,'x'=4,'yh'=2,'core'=2] {'z','yl','yh'}, dimensions={0} | all-to-all | bytes 2621440 | tf_op jit(solution)/shard_map/all_to_all | solution.py:333
  140.7 75.0 %shard_map.97 = (bf16[8,2,160,384]{3,2,1,0:T(8,128)(2,1)}, bf16[8,2,160,384]{3,2,1,0:T(8,128)(2,1)}, bf16[2560,256]{1,0:T(8,128)(2,1)}) custom-call(s32[1]{0:T(128)} %bitcast.yh_ref, bf16[8,2,160,384]{3,2,1,0:T(8,128)(2,1)} %copy-done, bf16[8,2,160,384]{3,2,1,0:T(8,128)(2,1)} %all-to-all-done.1.do_ref, bf16[2560,256]{1,0:T(8,128)(2,1)} %bitcast.28), custom_call_target="tpu_custom_call" | custom-call | tf_op jit(solution)/shard_map/pallas_call | solution.py:288
  215.7 22.3 %all_to_all.41 = bf16[16,160,256]{2,1,0:T(8,128)(2,1)S(1)} all-to-all(bf16[16,160,256]{2,1,0:T(8,128)(2,1)} %bitcast.33), channel_id=1, replica_groups=mesh['z'=4,'yl'=2,'x'=4,'yh'=2,'core'=2] {'z','yl','yh'}, dimensions={0} | all-to-all | bytes 2621440 | tf_op jit(solution)/shard_map/all_to_all | solution.py:333
  238.1 28.5 %all_to_all.42 = bf16[8,2,160,384]{3,2,1,0:T(8,128)(2,1)S(1)} all-to-all(bf16[8,2,160,384]{3,2,1,0:T(8,128)(2,1)S(1)} %copy-done.3), channel_id=1, replica_groups=mesh['z'=4,'yl'=2,'x'=4,'yh'=2,'core'=2] {'x','core'}, dimensions={0} | all-to-all | bytes 3932160 | tf_op jit(solution)/shard_map/all_to_all | solution.py:333
  266.5 4.3 %all-to-all-start.5 = ((bf16[8,2,160,384]{3,2,1,0:T(8,128)(2,1)}), bf16[8,2,160,384]{3,2,1,0:T(8,128)(2,1)}, u32[]{:S(2)}, u32[]{:S(2)}) async-start(bf16[8,2,160,384]{3,2,1,0:T(8,128)(2,1)} %get-tuple-element.11), calls=%async_computation.5 | async-start | bytes 3932160 | tf_op jit(solution)/shard_map/all_to_all | solution.py:333
  271.8 25.5 %all-to-all-done.5 = bf16[8,2,160,384]{3,2,1,0:T(8,128)(2,1)} async-done(((bf16[8,2,160,384]{3,2,1,0:T(8,128)(2,1)}), bf16[8,2,160,384]{3,2,1,0:T(8,128)(2,1)}, u32[]{:S(2)}, u32[]{:S(2)}) %all-to-all-start.5) | async-done | bytes 1966112 | tf_op jit(solution)/shard_map/all_to_all | solution.py:333
  298.2 7.1 %all-to-all-start.7 = ((bf16[8,160,256]{2,1,0:T(8,128)(2,1)}), bf16[8,160,256]{2,1,0:T(8,128)(2,1)S(1)}, u32[]{:S(2)}, u32[]{:S(2)}) async-start(bf16[8,160,256]{2,1,0:T(8,128)(2,1)} %broadcast_in_dim.5), calls=%async_computation.7 | async-start | bytes 1310720 | tf_op jit(solution)/shard_map/all_to_all | solution.py:333
  306.9 3.2 copy.21
  310.0 7.2 %all-to-all-done.7.g_ref = bf16[8,160,256]{2,1,0:T(8,128)(2,1)S(1)} async-done(((bf16[8,160,256]{2,1,0:T(8,128)(2,1)}), bf16[8,160,256]{2,1,0:T(8,128)(2,1)S(1)}, u32[]{:S(2)}, u32[]{:S(2)}) %all-to-all-start.7) | async-done | bytes 655392 | tf_op jit(solution)/shard_map/all_to_all | solution.py:333
  318.1 3.0 shard_map.98
  (39 shorter events, 18.4 us)
Async XLA Ops:
  4.4 6.6 %collective-permute-start.2 = (bf16[400,128]{1,0:T(8,128)(2,1)}, bf16[400,128]{1,0:T(8,128)(2,1)S(1)}, u32[]{:S(2)}, u32[]{:S(2)}) collective-permute-start(bf16[400,128]{1,0:T(8,128)(2,1)} %shard_map.94.own_ref), channel_id=1, source_target_pairs={{0,3},{1,2},{2,1},{3,0},{4,7},{5,6},{6,5},{7,4},{8,11},{9,10},{10,... | collective-permute-start | bytes 307208 | tf_op jit(solution)/shard_map/ppermute | solution.py:357
  7.1 7.2 %collective-permute-start.1 = (bf16[400,128]{1,0:T(8,128)(2,1)}, bf16[400,128]{1,0:T(8,128)(2,1)S(1)}, u32[]{:S(2)}, u32[]{:S(2)}) collective-permute-start(bf16[400,128]{1,0:T(8,128)(2,1)} %shard_map.94.own_ref), channel_id=1, source_target_pairs={{0,2},{1,3},{2,0},{3,1},{4,6},{5,7},{6,4},{7,5},{8,10},{9,11},{10,... | collective-permute-start | bytes 307208 | tf_op jit(solution)/shard_map/ppermute | solution.py:357
  7.7 6.6 %collective-permute-start = (bf16[400,128]{1,0:T(8,128)(2,1)}, bf16[400,128]{1,0:T(8,128)(2,1)S(1)}, u32[]{:S(2)}, u32[]{:S(2)}) collective-permute-start(bf16[400,128]{1,0:T(8,128)(2,1)} %shard_map.94.own_ref), channel_id=1, source_target_pairs={{0,1},{1,0},{2,3},{3,2},{4,5},{5,4},{6,7},{7,6},{8,9},{9,8},{10,11... | collective-permute-start | bytes 307208 | tf_op jit(solution)/shard_map/ppermute | solution.py:357
  11.0 3.4 %copy-start.4 = (bf16[400,128]{1,0:T(8,128)(2,1)}, bf16[400,128]{1,0:T(8,128)(2,1)S(1)}, u32[]{:S(2)}) copy-start(bf16[400,128]{1,0:T(8,128)(2,1)S(1)} %collective-permute-done.2.c_ref) | copy-start | bytes 307204
  14.3 0.6 copy-start.5
  14.3 0.7 copy-start.6
  16.9 7.4 %collective-permute-start.5 = (bf16[400,128]{1,0:T(8,128)(2,1)}, bf16[400,128]{1,0:T(8,128)(2,1)S(1)}, u32[]{:S(2)}, u32[]{:S(2)}) collective-permute-start(bf16[400,128]{1,0:T(8,128)(2,1)} %get-tuple-element.9), channel_id=1, source_target_pairs={{0,12},{4,0},{8,4},{12,8},{1,13},{5,1},{9,5},{13,9},{2,14},{6,2},{... | collective-permute-start | bytes 307208 | tf_op jit(solution)/shard_map/ppermute | solution.py:360
  19.7 7.2 %collective-permute-start.4 = (bf16[400,128]{1,0:T(8,128)(2,1)}, bf16[400,128]{1,0:T(8,128)(2,1)S(1)}, u32[]{:S(2)}, u32[]{:S(2)}) collective-permute-start(bf16[400,128]{1,0:T(8,128)(2,1)} %get-tuple-element.9), channel_id=1, source_target_pairs={{0,8},{4,12},{8,0},{12,4},{1,9},{5,13},{9,1},{13,5},{2,10},{6,14},... | collective-permute-start | bytes 307208 | tf_op jit(solution)/shard_map/ppermute | solution.py:360
  20.5 7.4 %collective-permute-start.3 = (bf16[400,128]{1,0:T(8,128)(2,1)}, bf16[400,128]{1,0:T(8,128)(2,1)S(1)}, u32[]{:S(2)}, u32[]{:S(2)}) collective-permute-start(bf16[400,128]{1,0:T(8,128)(2,1)} %get-tuple-element.9), channel_id=1, source_target_pairs={{0,4},{4,8},{8,12},{12,0},{1,5},{5,9},{9,13},{13,1},{2,6},{6,10},{... | collective-permute-start | bytes 307208 | tf_op jit(solution)/shard_map/ppermute | solution.py:360
  24.4 3.6 %copy-start.7 = (bf16[400,128]{1,0:T(8,128)(2,1)}, bf16[400,128]{1,0:T(8,128)(2,1)S(1)}, u32[]{:S(2)}) copy-start(bf16[400,128]{1,0:T(8,128)(2,1)S(1)} %collective-permute-done.5.c_ref) | copy-start | bytes 307204
  26.9 1.1 copy-start.8
  27.9 0.6 copy-start.9
  28.6 10.1 %copy-start.2 = (bf16[2,160,3072]{2,1,0:T(8,128)(2,1)S(1)}, bf16[2,160,3072]{2,1,0:T(8,128)(2,1)}, u32[]{:S(2)}) copy-start(bf16[2,160,3072]{2,1,0:T(8,128)(2,1)} %param.7) | copy-start | bytes 5898244
  33.0 16.9 %all-to-all-start.2 = ((bf16[8,160,256]{2,1,0:T(8,128)(2,1)}), bf16[8,160,256]{2,1,0:T(8,128)(2,1)S(1)}, u32[]{:S(2)}, u32[]{:S(2)}) async-start(bf16[8,160,256]{2,1,0:T(8,128)(2,1)} %shard_map.96), calls=%async_computation.2 | async-start | bytes 1310720 | tf_op jit(solution)/shard_map/all_to_all | solution.py:333
  49.9 29.3 %all-to-all-start = ((bf16[8,2,160,384]{3,2,1,0:T(8,128)(2,1)}), bf16[8,2,160,384]{3,2,1,0:T(8,128)(2,1)S(1)}, u32[]{:S(2)}, u32[]{:S(2)}) async-start(bf16[8,2,160,384]{3,2,1,0:T(8,128)(2,1)} %bitcast.27), calls=%async_computation | async-start | bytes 3932160 | tf_op jit(solution)/shard_map/all_to_all | solution.py:333
  79.2 1.3 copy-start
  80.5 30.7 %all-to-all-start.1 = ((bf16[8,2,160,384]{3,2,1,0:T(8,128)(2,1)}), bf16[8,2,160,384]{3,2,1,0:T(8,128)(2,1)}, u32[]{:S(2)}, u32[]{:S(2)}) async-start(bf16[8,2,160,384]{3,2,1,0:T(8,128)(2,1)} %bitcast.26), calls=%async_computation.1 | async-start | bytes 3932160 | tf_op jit(solution)/shard_map/all_to_all | solution.py:333
  84.9 0.7 collective-permute-start.6
  215.7 22.3 %copy-start.3 = (bf16[8,2,160,384]{3,2,1,0:T(8,128)(2,1)S(1)}, bf16[8,2,160,384]{3,2,1,0:T(8,128)(2,1)}, u32[]{:S(2)}) copy-start(bf16[8,2,160,384]{3,2,1,0:T(8,128)(2,1)} %get-tuple-element.10) | copy-start | bytes 5898244
  266.5 30.7 %all-to-all-start.5 = ((bf16[8,2,160,384]{3,2,1,0:T(8,128)(2,1)}), bf16[8,2,160,384]{3,2,1,0:T(8,128)(2,1)}, u32[]{:S(2)}, u32[]{:S(2)}) async-start(bf16[8,2,160,384]{3,2,1,0:T(8,128)(2,1)} %get-tuple-element.11), calls=%async_computation.5 | async-start | bytes 3932160 | tf_op jit(solution)/shard_map/all_to_all | solution.py:333
  271.1 0.7 collective-permute-start.7
  298.2 19.1 %all-to-all-start.7 = ((bf16[8,160,256]{2,1,0:T(8,128)(2,1)}), bf16[8,160,256]{2,1,0:T(8,128)(2,1)S(1)}, u32[]{:S(2)}, u32[]{:S(2)}) async-start(bf16[8,160,256]{2,1,0:T(8,128)(2,1)} %broadcast_in_dim.5), calls=%async_computation.7 | async-start | bytes 1310720 | tf_op jit(solution)/shard_map/all_to_all | solution.py:333
  317.2 0.9 copy-start.1
